TPU v7x, 32 devices: a whole 2x2x4 slice. The times are simulated.
32 devices in a mesh: groups: 1, expert: 32 (over z, y, x, core).
Axes of the slice: x: 2, y: 2, z: 4, core: 2. Of those that a mesh axis runs over, the one named last changes fastest.
Arguments:
- attn_heads: bfloat16 [32, 256, 256], P(('groups', 'expert')), may hold values from -6 to 6
- out_proj: bfloat16 [32, 256, 4096], P('expert'), may hold values from -0.09375 to 0.09375
- norm_gain: bfloat16 [4096], replicated, may hold values from 0.099609375 to 1.8984375
- routes: int32 [512, 8], P(('groups', 'expert')), may hold values from 0 to 15, all different within a row; in each aligned block of 16 rows (0 to 15, 16 to 31, ...) at most 16 rows name the same one
- gate_weights: float32 [512, 8], P(('groups', 'expert')), may hold values from 0.05 to 0.4
- expert_home: int32 [16], replicated, may hold values from 0 to 15, each once
- w_gate: bfloat16 [32, 4096, 384], P('expert'), may hold values from -0.09375 to 0.09375
- w_up: bfloat16 [32, 4096, 384], P('expert'), may hold values from -0.09375 to 0.09375
- w_down: bfloat16 [32, 384, 4096], P('expert'), may hold values from -0.21875 to 0.21875
Outputs:
- block_out: bfloat16 [512, 4096], P(('groups', 'expert'))
Inputs may be any that keep to these rules, and one draw needn't show every extreme that they name: `routes`: in each block of 16 rows (one device's tokens) no expert is named more than 16 times, a bound that some block reaches; a row names 8 different experts. `expert_home`: A permutation: each pair of devices holds exactly one expert.
All inputs are finite; a program needn't handle non-finite values.
Results may differ from a plain program's by a relative error of at most 0.014.
Values may be sent and summed in bfloat16 or wider, within the bound.
A program may use at most 128 MiB of HBM per device.

v0:
```python
import jax
import jax.numpy as jnp
from jax import lax
from jax.sharding import PartitionSpec as P

TP = 16


def from_partner(x, axis, bit):
    return lax.ppermute(x, axis, [(i, i ^ 1 << bit) for i in range(lax.axis_size(axis))])


def expert_act(rows_in, w_one, w_three):
    gate = jnp.dot(rows_in, w_one, preferred_element_type=jnp.float32)
    upper = jnp.dot(rows_in, w_three, preferred_element_type=jnp.float32)
    return (jax.nn.silu(gate) * upper).astype(jnp.bfloat16)


def body(attn_heads, out_proj, norm_gain, routes, gate_weights, expert_home, w_gate, w_up, w_down):
    width = out_proj.shape[2]
    rows_dev = routes.shape[0]
    top = routes.shape[1]
    experts_all = expert_home.shape[0]
    devices = lax.axis_size("expert")
    cap = min(rows_dev, 2 * rows_dev * top // experts_all)
    here = lax.axis_index("expert")
    side = here % 2
    levels = TP.bit_length() - 1
    partial_value = jnp.dot(attn_heads[0], out_proj[0], preferred_element_type=jnp.float32).astype(
        jnp.bfloat16
    )
    blocks = partial_value.reshape((2,) * levels + (rows_dev, width))
    order = list(range(levels - 1, -1, -1))
    remaining = list(range(levels - 1, -1, -1))
    for step, bit in enumerate(order):
        position = len([b for b in remaining if b > bit])
        remaining = [b for b in remaining if b != bit]
        keep = here >> bit & 1
        mine = lax.dynamic_index_in_dim(blocks, keep, position, keepdims=False)
        other = lax.dynamic_index_in_dim(blocks, 1 - keep, position, keepdims=False)
        if step == 0:
            got = from_partner(other, "expert", bit)
        else:
            got = from_partner(other.astype(jnp.bfloat16), "expert", bit).astype(other.dtype)
        blocks = mine.astype(jnp.float32) + got.astype(jnp.float32)
    scale = lax.rsqrt(jnp.mean(blocks * blocks, axis=-1, keepdims=True) + 1e-06)
    normed = (blocks * scale * norm_gain.astype(jnp.float32)).astype(jnp.bfloat16)
    flat = routes.reshape(-1)
    choose = (flat[:, None] == jnp.arange(experts_all, dtype=jnp.int32)[None, :]).astype(jnp.int32)
    earlier = jnp.cumsum(choose, axis=0) - choose
    slot = jnp.sum(earlier * choose, axis=1)
    home = jnp.sum(choose * expert_home[None, :], axis=1)
    target = home * cap + slot
    place = (target[:, None] == jnp.arange(experts_all * cap, dtype=jnp.int32)[None, :]).astype(
        jnp.bfloat16
    )
    owner = (
        jnp.arange(rows_dev * top, dtype=jnp.int32)[:, None] // top
        == jnp.arange(rows_dev, dtype=jnp.int32)[None, :]
    ).astype(jnp.bfloat16)
    select = jnp.einsum("ra,rt->at", place, owner, preferred_element_type=jnp.float32).astype(
        jnp.bfloat16
    )
    packed = jnp.dot(select, normed, preferred_element_type=jnp.float32).astype(jnp.bfloat16)
    own_in = jnp.stack([w_gate[0], w_up[0]])
    pair_in = from_partner(own_in, "expert", 0)
    pair_two = from_partner(w_down[0], "expert", 0)
    first_in = jnp.where(side == 0, own_in, pair_in)
    second_in = jnp.where(side == 0, pair_in, own_in)
    first_two = jnp.where(side == 0, w_down[0], pair_two)
    second_two = jnp.where(side == 0, pair_two, w_down[0])
    w_one = jnp.concatenate([first_in[0], second_in[0]], axis=1)
    w_three = jnp.concatenate([first_in[1], second_in[1]], axis=1)
    w_two = jnp.concatenate([first_two, second_two], axis=0)
    sent = (
        packed.reshape(experts_all, cap // 2, 2, width)
        .transpose(0, 2, 1, 3)
        .reshape(devices, cap // 2, width)
    )
    arrived = lax.all_to_all(sent, "expert", split_axis=0, concat_axis=0, tiled=True).reshape(
        devices * (cap // 2), width
    )
    act = expert_act(arrived, w_one, w_three)
    finished = jnp.dot(act, w_two, preferred_element_type=jnp.float32).astype(jnp.bfloat16)
    finished = finished.reshape(devices, cap // 2, width)
    back = lax.all_to_all(finished, "expert", split_axis=0, concat_axis=0, tiled=True)
    outputs = (
        back.reshape(experts_all, 2, cap // 2, width)
        .transpose(0, 2, 1, 3)
        .reshape(experts_all * cap, width)
    )
    picked = outputs[target].astype(jnp.float32).reshape(rows_dev, top, width)
    mixture = jnp.sum(picked * gate_weights[:, :, None], axis=1)
    return (blocks + mixture).astype(jnp.bfloat16)


def solution(mesh):
    placed = (
        P(("groups", "expert"), None, None),
        P("expert", None, None),
        P(),
        P(("groups", "expert"), None),
        P(("groups", "expert"), None),
        P(),
        P("expert", None, None),
        P("expert", None, None),
        P("expert", None, None),
    )
    return jax.shard_map(
        body, mesh=mesh, in_specs=placed, out_specs=P(("groups", "expert"), None), check_vma=False
    )
```

profile of v0, /device:TPU:0, one launch (start us, length us, event | category | flops | bytes accessed | tf_op | source)
XLA Modules:
  0.0 202.6 jit_solution(9646408703032942194)
XLA Ops:
  0.0 0.0 copy-start
  0.0 1.6 copy-done
  1.6 0.0 copy-start.6
  1.6 1.8 convolution_convert_fusion.1
  3.4 0.0 copy-start.2
  3.4 1.3 copy-done.2
  4.7 1.1 dynamic-slice_bitcast_fusion
  5.7 0.0 copy-start.7
  5.7 3.0 %collective-permute-start = (bf16[2,2,2,16,4096]{4,3,2,1,0:T(8,128)(2,1)}, bf16[2,2,2,16,4096]{4,3,2,1,0:T(8,128)(2,1)S(1)}, u32[]{:S(2)}, u32[]{:S(2)}) collective-permute-start(bf16[2,2,2,16,4096]{4,3,2,1,0:T(8,128)(2,1)} %dynamic-slice_bitcast_fusion), channel_id=1, source_target_pairs={{0,8},{1,9},{2,10},{3,11},{4,12},{5,13},{6,14},{7,15},{8,0},{9,1},... | collective-permute-start | bytes 3145736 | tf_op jit(solution)/shard_map/ppermute | solution.py:10
  8.8 0.0 copy-done.6
  8.8 2.0 constant_dynamic-update-slice_fusion.1
  10.8 0.0 copy-done.7
  10.8 0.0 copy-start.3
  10.8 2.0 constant_dynamic-update-slice_fusion
  12.8 0.0 copy-start.9
  12.8 0.0 collective-permute-start.4
  12.8 19.4 %collective-permute-done = bf16[2,2,2,16,4096]{4,3,2,1,0:T(8,128)(2,1)S(1)} collective-permute-done((bf16[2,2,2,16,4096]{4,3,2,1,0:T(8,128)(2,1)}, bf16[2,2,2,16,4096]{4,3,2,1,0:T(8,128)(2,1)S(1)}, u32[]{:S(2)}, u32[]{:S(2)}) %collective-permute-start) | collective-permute-done | bytes 1048608 | tf_op jit(solution)/shard_map/ppermute | solution.py:10
  32.1 0.0 copy-done.3
  32.1 0.2 convert_add_fusion
  32.4 0.0 copy-start.4
  32.4 1.3 copy-done.4
  33.7 0.0 copy-start.11
  33.7 0.1 fusion.22
  33.8 1.8 collective-permute-start.1
  35.5 0.0 collective-permute-start.5
  35.5 0.0 copy-done.9
  35.5 0.1 copy.13
  35.6 0.1 eq.24
  35.7 11.3 %collective-permute-done.1 = bf16[2,2,16,4096]{3,2,1,0:T(8,128)(2,1)S(1)} collective-permute-done((bf16[2,2,16,4096]{3,2,1,0:T(8,128)(2,1)S(1)}, bf16[2,2,16,4096]{3,2,1,0:T(8,128)(2,1)S(1)}, u32[]{:S(2)}, u32[]{:S(2)}) %collective-permute-start.1) | collective-permute-done | bytes 524320 | tf_op jit(solution)/shard_map/ppermute | solution.py:10
  47.0 1.3 bitcast_add_fusion
  48.3 1.4 collective-permute-start.2
  49.7 0.1 fusion.39
  49.8 0.2 reduce_window_sum.11
  50.0 0.0 copy-done.11
  50.0 0.2 select_reduce_fusion.1
  50.2 4.8 %collective-permute-done.2 = bf16[2,16,4096]{2,1,0:T(8,128)(2,1)S(1)} collective-permute-done((bf16[2,16,4096]{2,1,0:T(8,128)(2,1)S(1)}, bf16[2,16,4096]{2,1,0:T(8,128)(2,1)S(1)}, u32[]{:S(2)}, u32[]{:S(2)}) %collective-permute-start.2) | collective-permute-done | bytes 262176 | tf_op jit(solution)/shard_map/ppermute | solution.py:10
  55.0 0.0 copy-start.5
  55.0 0.1 collective-permute-start.3
  55.1 0.0 copy-done.8
  55.2 1.3 collective-permute-done.3
  56.5 0.2 multiply_reduce_fusion
  56.6 1.0 convolution_convert_fusion
  57.6 2.7 %reshape.110 = bf16[16,8,2,4096]{3,2,1,0:T(2,128)(2,1)} reshape(bf16[256,4096]{1,0:T(8,128)(2,1)S(1)} %convolution_convert_fusion) | data formatting | bytes 4194304 | tf_op jit(solution)/shard_map/reshape | solution.py:76
  60.2 0.0 copy-done.5
  60.2 4.2 %copy.14 = bf16[16,8,2,4096]{3,1,2,0:T(8,128)(2,1)} copy(bf16[16,8,2,4096]{3,2,1,0:T(2,128)(2,1)} %reshape.110) | data formatting | bytes 4194304 | tf_op jit(solution)/shard_map/reshape | solution.py:76
  64.5 5.7 %all-to-all-start = ((bf16[32,8,4096]{2,1,0:T(8,128)(2,1)}), bf16[32,8,4096]{2,1,0:T(8,128)(2,1)S(1)}, u32[]{:S(2)}, u32[]{:S(2)}) async-start(bf16[32,8,4096]{2,1,0:T(8,128)(2,1)} %bitcast.12), calls=%async_computation | async-start | bytes 4194304 | tf_op jit(solution)/shard_map/all_to_all | solution.py:80
  70.2 0.0 collective-permute-done.5
  70.2 5.8 %broadcast_select_fusion.3 = (bf16[384,4096]{1,0:T(8,128)(2,1)}, bf16[384,4096]{1,0:T(8,128)(2,1)}) fusion(bf16[384,4096]{1,0:T(8,128)(2,1)} %collective-permute-done.5, pred[]{:T(512)S(6)} %eq.59, bf16[1,384,4096]{2,1,0:T(8,128)(2,1)} %param.17), kind=kLoop, calls=%fused_computation.24 | loop fusion | flops 3145728 | bytes 12582913 | tf_op jit(solution)/shard_map/jit(_where)/select_n | solution.py:70
  76.0 0.0 collective-permute-done.4
  76.0 5.7 %broadcast_select_fusion.1 = (bf16[2,4096,384]{2,1,0:T(8,128)(2,1)S(1)}, bf16[2,4096,384]{2,1,0:T(8,128)(2,1)S(1)}) fusion(bf16[2,4096,384]{2,1,0:T(8,128)(2,1)} %constant_dynamic-update-slice_fusion, bf16[2,4096,384]{2,1,0:T(8,128)(2,1)} %collective-permute-done.4, pred[]{:T(512)S(6)} %eq.59), kind=kLoop, calls=%fused_computation.14 | loop fusion | flops 6291456 | bytes 25165824 | tf_op jit(solution)/shard_map/jit(_where)/select_n | solution.py:68
  81.7 4.8 %slice_bitcast_fusion = (bf16[4096,384]{1,0:T(8,128)(2,1)}, bf16[4096,384]{1,0:T(8,128)(2,1)}, bf16[4096,384]{1,0:T(8,128)(2,1)}, bf16[4096,384]{1,0:T(8,128)(2,1)}) fusion(bf16[2,4096,384]{2,1,0:T(8,128)(2,1)S(1)} %get-tuple-element.10, bf16[2,4096,384]{2,1,0:T(8,128)(2,1)S(1)} %get-tuple-element.9), kind=kLoop, calls=%fused_computation.19 | loop fusion | bytes 25165824 | tf_op jit(solution)/shard_map/squeeze | solution.py:73
  86.5 32.5 %all-to-all-done = bf16[32,8,4096]{2,1,0:T(8,128)(2,1)S(1)} async-done(((bf16[32,8,4096]{2,1,0:T(8,128)(2,1)}), bf16[32,8,4096]{2,1,0:T(8,128)(2,1)S(1)}, u32[]{:S(2)}, u32[]{:S(2)}) %all-to-all-start) | async-done | bytes 2097184 | tf_op jit(solution)/shard_map/all_to_all | solution.py:80
  119.0 5.5 %fusion = f32[256,768]{1,0:T(8,128)} fusion(bf16[4096,384]{1,0:T(8,128)(2,1)} %get-tuple-element.14, bf16[4096,384]{1,0:T(8,128)(2,1)} %get-tuple-element.17, bf16[32,8,4096]{2,1,0:T(8,128)(2,1)S(1)} %all-to-all-done), kind=kOutput, calls=%fused_computation.1 | convolution fusion | flops 1623195648 | bytes 9175040 | tf_op jit(solution)/shard_map/dot_general | solution.py:14
  124.5 10.8 %fusion.15 = bf16[32,8,4096]{2,1,0:T(8,128)(2,1)} fusion(bf16[384,4096]{1,0:T(8,128)(2,1)} %get-tuple-element.16, bf16[384,4096]{1,0:T(8,128)(2,1)} %get-tuple-element.15, f32[256,768]{1,0:T(8,128)} %fusion, bf16[4096,384]{1,0:T(8,128)(2,1)} %get-tuple-element.13, bf16[4096,384]{1,0:T(8,128)(2,1)} %get-tuple-element.18, ...), kind=kOutput, calls=%fused_computation.18 | convolution fusion | flops 3248619520 | bytes 17563648 | tf_op jit(solution)/shard_map/dot_general | solution.py:84
  135.2 4.2 %all-to-all-start.1 = ((bf16[32,8,4096]{2,1,0:T(8,128)(2,1)}), bf16[32,8,4096]{2,1,0:T(8,128)(2,1)S(1)}, u32[]{:S(2)}, u32[]{:S(2)}) async-start(bf16[32,8,4096]{2,1,0:T(8,128)(2,1)} %fusion.15), calls=%async_computation.1 | async-start | bytes 4194304 | tf_op jit(solution)/shard_map/all_to_all | solution.py:86
  139.4 0.0 copy-done.10
  139.4 0.1 copy.16
  139.5 48.7 %all-to-all-done.1 = bf16[32,8,4096]{2,1,0:T(8,128)(2,1)S(1)} async-done(((bf16[32,8,4096]{2,1,0:T(8,128)(2,1)}), bf16[32,8,4096]{2,1,0:T(8,128)(2,1)S(1)}, u32[]{:S(2)}, u32[]{:S(2)}) %all-to-all-start.1) | async-done | bytes 2097184 | tf_op jit(solution)/shard_map/all_to_all | solution.py:86
  188.2 3.6 %copy.18 = bf16[16,2,8,4096]{3,1,2,0:T(2,128)(2,1)} copy(bf16[16,2,8,4096]{3,2,1,0:T(8,128)(2,1)S(1)} %bitcast.69) | data formatting | bytes 4194304 | tf_op jit(solution)/shard_map/reshape | solution.py:88
  191.8 4.1 %reshape.115 = bf16[256,4096]{1,0:T(8,128)(2,1)} reshape(bf16[16,8,2,4096]{3,2,1,0:T(2,128)(2,1)} %bitcast.70) | data formatting | bytes 4194304 | tf_op jit(solution)/shard_map/reshape | solution.py:90
  195.9 4.2 %gather_fusion = bf16[128,4096]{1,0:T(8,128)(2,1)S(1)} fusion(bf16[256,4096]{1,0:T(8,128)(2,1)} %reshape.115, s32[1024]{0:T(1024)S(1)} %pad_clamp_fusion), kind=kCustom, calls=%fused_computation | custom fusion | bytes 2097664 | tf_op jit(solution)/shard_map/gather | solution.py:92
  200.1 0.8 fusion.18
  200.9 1.7 add_convert_fusion
  202.6 0.0 copy-done.1
  (11 shorter events, 0.1 us)
Async XLA Ops:
  0.0 1.6 copy-start
  1.6 7.2 %copy-start.6 = (bf16[1,4096,384]{2,1,0:T(8,128)(2,1)S(1)}, bf16[1,4096,384]{2,1,0:T(8,128)(2,1)}, u32[]{:S(2)}) copy-start(bf16[1,4096,384]{2,1,0:T(8,128)(2,1)} %param.15) | copy-start | bytes 9437188
  3.4 1.3 copy-start.2
  5.7 5.1 %copy-start.7 = (bf16[1,4096,384]{2,1,0:T(8,128)(2,1)S(1)}, bf16[1,4096,384]{2,1,0:T(8,128)(2,1)}, u32[]{:S(2)}) copy-start(bf16[1,4096,384]{2,1,0:T(8,128)(2,1)} %param.16) | copy-start | bytes 9437188
  5.7 26.4 %collective-permute-start = (bf16[2,2,2,16,4096]{4,3,2,1,0:T(8,128)(2,1)}, bf16[2,2,2,16,4096]{4,3,2,1,0:T(8,128)(2,1)S(1)}, u32[]{:S(2)}, u32[]{:S(2)}) collective-permute-start(bf16[2,2,2,16,4096]{4,3,2,1,0:T(8,128)(2,1)} %dynamic-slice_bitcast_fusion), channel_id=1, source_target_pairs={{0,8},{1,9},{2,10},{3,11},{4,12},{5,13},{6,14},{7,15},{8,0},{9,1},... | collective-permute-start | bytes 3145736 | tf_op jit(solution)/shard_map/ppermute | solution.py:10
  10.8 21.3 %copy-start.3 = (bf16[256,4096]{1,0:T(8,128)(2,1)S(1)}, bf16[256,4096]{1,0:T(8,128)(2,1)}, u32[]{:S(2)}) copy-start(bf16[256,4096]{1,0:T(8,128)(2,1)} %copy-done.2) | copy-start | bytes 6291460
  12.8 22.8 %copy-start.9 = (s32[16,8]{0,1:T(8,128)S(1)}, s32[16,8]{0,1:T(8,128)}, u32[]{:S(2)}) copy-start(s32[16,8]{0,1:T(8,128)} %param.12) | copy-start | bytes 1540
  12.8 63.3 %collective-permute-start.4 = (bf16[2,4096,384]{2,1,0:T(8,128)(2,1)}, bf16[2,4096,384]{2,1,0:T(8,128)(2,1)}, u32[]{:S(2)}, u32[]{:S(2)}) collective-permute-start(bf16[2,4096,384]{2,1,0:T(8,128)(2,1)} %constant_dynamic-update-slice_fusion), channel_id=1, source_target_pairs={{0,1},{1,0},{2,3},{3,2},{4,5},{5,4},{6,7},{7,6},{8,9},{9,8},{10,11... | collective-permute-start | bytes 18874376 | tf_op jit(solution)/shard_map/ppermute | solution.py:10
  32.4 1.3 copy-start.4
  33.7 16.3 %copy-start.11 = (s32[16]{0:T(128)S(1)}, s32[16]{0:T(128)}, u32[]{:S(2)}) copy-start(s32[16]{0:T(128)} %param.14) | copy-start | bytes 196
  33.7 21.4 %copy-start.8 = (bf16[4096]{0:T(1024)(128)(2,1)S(1)}, bf16[4096]{0:T(1024)(128)(2,1)}, u32[]{:S(2)}) copy-start(bf16[4096]{0:T(1024)(128)(2,1)} %param.11) | copy-start | bytes 24580
  33.8 13.2 %collective-permute-start.1 = (bf16[2,2,16,4096]{3,2,1,0:T(8,128)(2,1)S(1)}, bf16[2,2,16,4096]{3,2,1,0:T(8,128)(2,1)S(1)}, u32[]{:S(2)}, u32[]{:S(2)}) collective-permute-start(bf16[2,2,16,4096]{3,2,1,0:T(8,128)(2,1)S(1)} %fusion.22), channel_id=1, source_target_pairs={{0,4},{1,5},{2,6},{3,7},{4,0},{5,1},{6,2},{7,3},{8,12},{9,13},{10,... | collective-permute-start | bytes 1572872 | tf_op jit(solution)/shard_map/ppermute | solution.py:10
  35.5 34.7 %collective-permute-start.5 = (bf16[384,4096]{1,0:T(8,128)(2,1)}, bf16[384,4096]{1,0:T(8,128)(2,1)}, u32[]{:S(2)}, u32[]{:S(2)}) collective-permute-start(bf16[384,4096]{1,0:T(8,128)(2,1)} %bitcast.18), channel_id=1, source_target_pairs={{0,1},{1,0},{2,3},{3,2},{4,5},{5,4},{6,7},{7,6},{8,9},{9,8},{10,11... | collective-permute-start | bytes 9437192 | tf_op jit(solution)/shard_map/ppermute | solution.py:10
  48.3 6.6 %collective-permute-start.2 = (bf16[2,16,4096]{2,1,0:T(8,128)(2,1)S(1)}, bf16[2,16,4096]{2,1,0:T(8,128)(2,1)S(1)}, u32[]{:S(2)}, u32[]{:S(2)}) collective-permute-start(bf16[2,16,4096]{2,1,0:T(8,128)(2,1)S(1)} %fusion.32), channel_id=1, source_target_pairs={{0,2},{1,3},{2,0},{3,1},{4,6},{5,7},{6,4},{7,5},{8,10},{9,11},{10,... | collective-permute-start | bytes 786440 | tf_op jit(solution)/shard_map/ppermute | solution.py:10
  55.0 5.2 %copy-start.5 = (f32[2,16,4096]{2,1,0:T(8,128)}, f32[2,16,4096]{2,1,0:T(8,128)S(1)}, u32[]{:S(2)}) copy-start(f32[2,16,4096]{2,1,0:T(8,128)S(1)} %bitcast_add_fusion.1) | copy-start | bytes 1572868
  55.0 1.4 collective-permute-start.3
  64.5 54.5 %all-to-all-start = ((bf16[32,8,4096]{2,1,0:T(8,128)(2,1)}), bf16[32,8,4096]{2,1,0:T(8,128)(2,1)S(1)}, u32[]{:S(2)}, u32[]{:S(2)}) async-start(bf16[32,8,4096]{2,1,0:T(8,128)(2,1)} %bitcast.12), calls=%async_computation | async-start | bytes 4194304 | tf_op jit(solution)/shard_map/all_to_all | solution.py:80
  135.2 4.2 %copy-start.10 = (f32[16,8]{0,1:T(8,128)S(1)}, f32[16,8]{0,1:T(8,128)}, u32[]{:S(2)}) copy-start(f32[16,8]{0,1:T(8,128)} %param.13) | copy-start | bytes 1540
  135.2 52.9 %all-to-all-start.1 = ((bf16[32,8,4096]{2,1,0:T(8,128)(2,1)}), bf16[32,8,4096]{2,1,0:T(8,128)(2,1)S(1)}, u32[]{:S(2)}, u32[]{:S(2)}) async-start(bf16[32,8,4096]{2,1,0:T(8,128)(2,1)} %fusion.15), calls=%async_computation.1 | async-start | bytes 4194304 | tf_op jit(solution)/shard_map/all_to_all | solution.py:86
  195.9 6.7 %copy-start.1 = (bf16[1,256,4096]{2,1,0:T(8,128)(2,1)S(1)}, bf16[1,256,4096]{2,1,0:T(8,128)(2,1)}, u32[]{:S(2)}) copy-start(bf16[1,256,4096]{2,1,0:T(8,128)(2,1)} %param.10) | copy-start | bytes 6291460
where the time goes:
time: 203 us
  waiting for transfers between devices  118 us (58%)
  local copies, waits for them, and re-layouts  33.2 us (16%)
  matrix products  19 us (9%)
  other arithmetic  16.2 us (8%)
  starting transfers between devices  16.1 us (8%)
    all_to_all x1, waiting for transfers between devices, body(): lax.all_to_all(finished, 'expert', split_axis=0, concat_axis=0, tiled=True)  48.7 us
    ppermute x6, waiting for transfers between devices, from_partner(): lax.ppermute(x, axis, [(i, i ^ 1 << bit) for i in range(lax.axis_size(axi...  36.7 us
    all_to_all x1, waiting for transfers between devices, body(): lax.all_to_all(sent, 'expert', split_axis=0, concat_axis=0, tiled=True)  32.5 us
    dot_general x1, matrix products, body(): jnp.dot(act, w_two, preferred_element_type=jnp.float32).astype(jnp.bfloat16)  10.8 us
    reshape x2, local copies, waits for them, and re-layouts, body(): packed.reshape(experts_all, cap // 2, 2, width).transpose(0, 2, 1, 3)  6.9 us
    unnamed x27, local copies, waits for them, and re-layouts  6.41 us
    ppermute x6, starting transfers between devices, from_partner(): lax.ppermute(x, axis, [(i, i ^ 1 << bit) for i in range(lax.axis_size(axi...  6.25 us
    select_n x1, other arithmetic, body(): first_two = jnp.where(side == 0, w_down[0], pair_two)  5.84 us
  transfers between devices with their start and end apart: 8, of which 6 were waited for; matrix products, arithmetic and copies ran while one was open for 15% of the time, Pallas kernels for 0%

commit v1 on v0

v1 whole, which is shorter than its diff:
```python
import jax
import jax.numpy as jnp
from jax import lax
from jax.sharding import PartitionSpec as P

TP = 16


def body(attn_heads, out_proj, norm_gain, routes, gate_weights, expert_home, w_gate, w_up, w_down):
    devices = lax.axis_size("expert")
    here = lax.axis_index("expert")
    experts_all = expert_home.shape[0]
    groups = [list(range(g * TP, (g + 1) * TP)) for g in range(devices // TP)]
    partial_value = jnp.dot(attn_heads[0], out_proj[0], preferred_element_type=jnp.float32).astype(
        jnp.bfloat16
    )
    state = lax.psum_scatter(
        partial_value, "expert", scatter_dimension=0, axis_index_groups=groups, tiled=True
    ).astype(jnp.float32)
    scale = lax.rsqrt(jnp.mean(state * state, axis=-1, keepdims=True) + 1e-06)
    normed = (state * scale * norm_gain.astype(jnp.float32)).astype(jnp.bfloat16)
    mine = routes[:, :, None] == jnp.arange(experts_all, dtype=jnp.int32)
    dense = jnp.sum(jnp.where(mine, gate_weights[:, :, None], 0.0), axis=1)
    dense = lax.all_gather(dense, "expert", axis=0, tiled=True)
    gate_here = jnp.sum(jnp.where(expert_home[None, :] == here // 2, dense, 0.0), axis=1, keepdims=True)
    rows = lax.all_gather(normed, "expert", axis=0, tiled=True)
    gate = jnp.dot(rows, w_gate[0], preferred_element_type=jnp.float32)
    upper = jnp.dot(rows, w_up[0], preferred_element_type=jnp.float32)
    act = (jax.nn.silu(gate) * upper).astype(jnp.bfloat16)
    part = jnp.dot(act, w_down[0], preferred_element_type=jnp.float32) * gate_here
    mixture = lax.psum_scatter(
        part.astype(jnp.bfloat16), "expert", scatter_dimension=0, tiled=True
    ).astype(jnp.float32)
    return (state + mixture).astype(jnp.bfloat16)


def solution(mesh):
    placed = (
        P(("groups", "expert"), None, None),
        P("expert", None, None),
        P(),
        P(("groups", "expert"), None),
        P(("groups", "expert"), None),
        P(),
        P("expert", None, None),
        P("expert", None, None),
        P("expert", None, None),
    )
    return jax.shard_map(
        body, mesh=mesh, in_specs=placed, out_specs=P(("groups", "expert"), None), check_vma=False
    )
```

time: 203 us -> 300 us (1.48)
  waiting for transfers between devices: 118 us -> 222 us
  blocking collectives: 0 us -> 39 us
  local copies, waits for them, and re-layouts: 33.2 us -> 0.17 us
  starting transfers between devices: 16.1 us -> 0.12 us
  between operations: 0.22 us -> 13.2 us
  other arithmetic: 16.2 us -> 4.59 us
    reduce_scatter x0 -> x2, waiting for transfers between devices: none -> 201 us  [the longest x1 139 us: body(): lax.psum_scatter(part.astype(jnp.bfloat16), 'expert', scatter_dimension=0...]
    all_to_all x2 -> x0, waiting for transfers between devices: 81.1 us -> none  [the longest x1 48.7 us: body(): lax.all_to_all(finished, 'expert', split_axis=0, concat_axis=0, tiled=True)]
    all_gather x0 -> x1, blocking collectives: none -> 39 us  [body(): dense = lax.all_gather(dense, 'expert', axis=0, tiled=True)]
    ppermute x6 -> x0, waiting for transfers between devices: 36.7 us -> none  [from_partner(): lax.ppermute(x, axis, [(i, i ^ 1 << bit) for i in range(lax.axis_size(axi...]
    all_gather x0 -> x1, waiting for transfers between devices: none -> 21.3 us  [body(): rows = lax.all_gather(normed, 'expert', axis=0, tiled=True)]
    reshape x4 -> x0, local copies, waits for them, and re-layouts: 14.6 us -> none  [the longest x2 6.9 us: body(): packed.reshape(experts_all, cap // 2, 2, width).transpose(0, 2, 1, 3)]
    select_n x4 -> x0, other arithmetic: 11.6 us -> none  [the longest x1 5.84 us: body(): first_two = jnp.where(side == 0, w_down[0], pair_two)]
    all_to_all x2 -> x0, starting transfers between devices: 9.86 us -> none  [the longest x1 5.68 us: body(): lax.all_to_all(sent, 'expert', split_axis=0, concat_axis=0, tiled=True)]
  transfers between devices with their start and end apart: 8 -> 3, of which waited for: 6 -> 3; matrix products, arithmetic and copies ran while one was open for 15% -> 0% of each run, Pallas kernels for 0% -> 0%
where the time goes in v1:
time: 300 us; the launch traced here: 299 us
  waiting for transfers between devices  222 us (74%)
  blocking collectives  39 us (13%)
  matrix products  20 us (7%)
  between operations  13.2 us (4%)
  other arithmetic  4.59 us (2%)
    reduce_scatter x1, waiting for transfers between devices, body(): lax.psum_scatter(part.astype(jnp.bfloat16), 'expert', scatter_dimension=0...  139 us
    reduce_scatter x1, waiting for transfers between devices, body(): lax.psum_scatter(partial_value, 'expert', scatter_dimension=0, axis_index...  61.5 us
    all_gather x1, blocking collectives, body(): dense = lax.all_gather(dense, 'expert', axis=0, tiled=True)  39 us
    all_gather x1, waiting for transfers between devices, body(): rows = lax.all_gather(normed, 'expert', axis=0, tiled=True)  21.3 us
    dot_general x1, matrix products, body(): jnp.dot(act, w_down[0], preferred_element_type=jnp.float32) * gate_here  9.73 us
    dot_general x1, matrix products, body(): gate = jnp.dot(rows, w_gate[0], preferred_element_type=jnp.float32)  6.43 us
  transfers between devices with their start and end apart: 3, of which 3 were waited for; matrix products, arithmetic and copies ran while one was open for 0% of the time, Pallas kernels for 0%

profile of v1, /device:TPU:0, one launch (start us, length us, event | category | flops | bytes accessed | tf_op | source)
XLA Modules:
  0.0 299.3 jit_solution(13494929814366687138)
XLA Ops:
  6.5 0.0 copy-start
  6.5 0.0 copy-start.2
  6.5 0.0 copy-start.3
  6.5 0.0 copy-start.4
  6.5 0.0 copy-start.5
  6.5 0.0 reduce-scatter.3.cloned.1.call-start
  6.6 3.9 %convolution_convert_fusion = bf16[256,4096]{1,0:T(8,128)(2,1)} fusion(bf16[1,256,4096]{2,1,0:T(8,128)(2,1)} %param.10, bf16[1,256,256]{2,1,0:T(8,128)(2,1)} %param.9), kind=kOutput, calls=%fused_computation.1 | convolution fusion | flops 537919488 | bytes 4325376 | tf_op jit(solution)/shard_map/dot_general | solution.py:14
  10.5 0.0 reduce-scatter.3.cloned.1.call-update
  10.5 0.0 all-gather.2.cloned.1.call-start
  10.5 0.0 copy-done.2
  10.6 61.5 %reduce-scatter.3.cloned.1.call-done = bf16[16,4096]{1,0:T(8,128)(2,1)} async-done(((bf16[256,4096]{1,0:T(8,128)(2,1)}), bf16[16,4096]{1,0:T(8,128)(2,1)}) %reduce-scatter.3.cloned.1.call-update) | async-done | bytes 131088 | tf_op jit(solution)/shard_map/reduce_scatter | solution.py:17
  72.0 1.0 fusion.15
  73.1 1.7 fusion.17
  74.8 0.0 all-gather.2.cloned.1.call-update
  74.8 0.0 reduce-scatter.5.cloned.1.call-start
  74.8 0.0 copy-done.3
  74.8 0.1 copy.12
  74.9 0.0 copy-done.4
  74.9 0.1 copy.13
  75.0 0.1 select_reduce_fusion.1
  75.1 39.0 %all_gather.7 = f32[512,16]{1,0:T(8,128)S(1)} all-gather(f32[16,16]{1,0:T(8,128)S(1)} %select_reduce_fusion.1), channel_id=1, replica_groups=mesh['groups'=1,'expert'=32] {'expert'}, dimensions={0}, use_global_device_ids=true | all-gather | bytes 33792 | tf_op jit(solution)/shard_map/all_gather | solution.py:24
  114.1 0.0 copy-done.5
  114.2 0.2 select_reduce_fusion
  114.3 21.3 %all-gather.2.cloned.1.call-done = bf16[512,4096]{1,0:T(8,128)(2,1)} async-done(((bf16[16,4096]{1,0:T(8,128)(2,1)}), bf16[512,4096]{1,0:T(8,128)(2,1)}) %all-gather.2.cloned.1.call-update) | async-done | bytes 4194320 | tf_op jit(solution)/shard_map/all_gather | solution.py:26
  135.6 6.4 %fusion.3 = f32[512,384]{1,0:T(8,128)} fusion(bf16[512,4096]{1,0:T(8,128)(2,1)} %all-gather.2.cloned.1.call-done, bf16[1,4096,384]{2,1,0:T(8,128)(2,1)} %param.15), kind=kOutput, calls=%fused_computation.5 | convolution fusion | flops 1610612736 | bytes 8126464 | tf_op jit(solution)/shard_map/dot_general | solution.py:27
  142.0 0.0 copy-done
  142.0 9.7 %multiply_convert_fusion = bf16[512,4096]{1,0:T(8,128)(2,1)} fusion(f32[512]{0:T(512)S(1)} %select_reduce_fusion, bf16[1,384,4096]{2,1,0:T(8,128)(2,1)S(1)} %copy-done, bf16[512,4096]{1,0:T(8,128)(2,1)} %all-gather.2.cloned.1.call-done, bf16[1,4096,384]{2,1,0:T(8,128)(2,1)} %param.16, f32[512,384]{1,0:T(8,128)} %fusion.3), kind=kOutput, calls=%fused_computation | convolution fusion | flops 3226599424 | bytes 15468544 | tf_op jit(solution)/shard_map/dot_general | solution.py:30
  151.7 0.0 copy-start.1
  151.7 0.0 reduce-scatter.5.cloned.1.call-update
  151.8 139.4 %reduce-scatter.5.cloned.1.call-done = bf16[16,4096]{1,0:T(8,128)(2,1)} async-done(((bf16[512,4096]{1,0:T(8,128)(2,1)}), bf16[16,4096]{1,0:T(8,128)(2,1)}) %reduce-scatter.5.cloned.1.call-update) | async-done | bytes 131088 | tf_op jit(solution)/shard_map/reduce_scatter | solution.py:31
  291.2 0.0 copy-done.1
  291.2 1.6 fusion.18
  (3 shorter events, 0.0 us)
Async XLA Ops:
  6.5 135.5 %copy-start = (bf16[1,384,4096]{2,1,0:T(8,128)(2,1)S(1)}, bf16[1,384,4096]{2,1,0:T(8,128)(2,1)}, u32[]{:S(2)}) copy-start(bf16[1,384,4096]{2,1,0:T(8,128)(2,1)} %param.17) | copy-start | bytes 9437188
  6.5 4.0 %copy-start.2 = (bf16[4096]{0:T(1024)(128)(2,1)S(1)}, bf16[4096]{0:T(1024)(128)(2,1)}, u32[]{:S(2)}) copy-start(bf16[4096]{0:T(1024)(128)(2,1)} %param.11) | copy-start | bytes 24580
  6.5 68.3 %copy-start.3 = (s32[16,8]{0,1:T(8,128)S(1)}, s32[16,8]{0,1:T(8,128)}, u32[]{:S(2)}) copy-start(s32[16,8]{0,1:T(8,128)} %param.12) | copy-start | bytes 1540
  6.5 68.4 %copy-start.4 = (f32[16,8]{0,1:T(8,128)S(1)}, f32[16,8]{0,1:T(8,128)}, u32[]{:S(2)}) copy-start(f32[16,8]{0,1:T(8,128)} %param.13) | copy-start | bytes 1540
  6.5 107.6 %copy-start.5 = (s32[16]{0:T(128)S(1)}, s32[16]{0:T(128)}, u32[]{:S(2)}) copy-start(s32[16]{0:T(128)} %param.14) | copy-start | bytes 196
  6.5 65.5 %reduce-scatter.3.cloned.1.call-start = ((), (), s32[]{:S(2)}) async-start(), calls=%async_computation.2 | async-start | bytes 2228224 | tf_op jit(solution)/shard_map/reduce_scatter | solution.py:17
  10.5 125.1 %all-gather.2.cloned.1.call-start = ((), (), s32[]{:S(2)}) async-start(), calls=%async_computation.3 | async-start | bytes 4325376 | tf_op jit(solution)/shard_map/all_gather | solution.py:26
  74.8 216.4 %reduce-scatter.5.cloned.1.call-start = ((), (), s32[]{:S(2)}) async-start(), calls=%async_computation.4 | async-start | bytes 4325376 | tf_op jit(solution)/shard_map/reduce_scatter | solution.py:31
  151.7 139.5 %copy-start.1 = (bf16[16,4096]{1,0:T(8,128)(2,1)S(1)}, bf16[16,4096]{1,0:T(8,128)(2,1)}, u32[]{:S(2)}) copy-start(bf16[16,4096]{1,0:T(8,128)(2,1)} %reduce-scatter.3.cloned.1.call-done) | copy-start | bytes 393220
Sparse Core Ops, SparseCore 0:
  10.6 61.3 reduce-scatter.2
  74.9 60.6 all-gather.1
  151.9 139.2 reduce-scatter.4

commit v2 on v1

v2 whole, which is shorter than its diff:
```python
import functools
import jax
import jax.numpy as jnp
from jax import lax
from jax.experimental import pallas as pl
from jax.experimental.pallas import tpu as pltpu
from jax.sharding import PartitionSpec as P

LANES = 128
STRIDE = 2
OFFSETS = {"first": 0, "relay": 1, "corner": 2, "expert": 3, "sum": 4, "second": 5, "home": 6}


def kernel(slabs, a_ref, wo_hbm, gain_ref, dense_ref, wg_hbm, wu_hbm, wd_hbm, out_ref, wo, w, wd,
           part, part_send, part_recv, t1_send, t1_recv, keep1, t2_send, t2_recv, keep2, t3_send,
           t3_recv, state, rows, hidden, y, y_send, y_recv, v1_send, v1_recv, v2_send, v2_recv,
           keep3, v3_send, v3_recv, load_sem, ps, pr, t1s, t1r, t2s, t2r, t3s, t3r, zs, zr, fs, fr,
           ds, dr, cs, cr, ys, yr, v1s, v1r, v2s, v2r, v3s, v3r):
    f32, bf16 = jnp.float32, jnp.bfloat16
    me = lax.axis_index("expert")
    q = me // 8
    yy = (me // 4) % 2
    xx = (me // 2) % 2
    cc = me % 2
    low = q % 2
    inner = me % 8
    core = me + 1 - 2 * cc
    xnbr = me + 2 - 4 * xx
    ynbr = me + 4 - 8 * yy
    znbr = me + 8 - 16 * low
    half = wo.shape[1] // 2
    units = wd.shape[0]
    rows_dev = out_ref.shape[0]
    first_nbr, second_nbr = (ynbr, xnbr), (xnbr, ynbr)
    second_at = (xx, yy)

    loads = [pltpu.make_async_copy(wo_hbm, wo, load_sem.at[0]),
             pltpu.make_async_copy(wg_hbm, w.at[:, 0:units], load_sem.at[1]),
             pltpu.make_async_copy(wu_hbm, w.at[:, units:2 * units], load_sem.at[2]),
             pltpu.make_async_copy(wd_hbm, wd, load_sem.at[3])]
    for load in loads:
        load.start()

    def slab_at(k):
        return lax.rem(q + k, slabs)

    barrier = pltpu.get_barrier_semaphore()
    others = [core, xnbr, ynbr] + [slab_at(k) * 8 + inner for k in range(1, slabs)]
    for other in others:
        pl.semaphore_signal(barrier, inc=1, device_id={"expert": other},
                            device_id_type=pl.DeviceIdType.MESH)

    sent = []

    def copy(src, dst, send_sem, recv_sem, device):
        return pltpu.make_async_remote_copy(
            src_ref=src, dst_ref=dst, send_sem=send_sem, recv_sem=recv_sem,
            device_id={"expert": device}, device_id_type=pl.DeviceIdType.MESH)

    def send(*args):
        made = copy(*args)
        made.start()
        sent.append(made)

    def wait(*args):
        copy(*args).wait_recv()

    loads[0].wait()
    chunk = min(512, half)
    heads = a_ref[...].reshape(16 * rows_dev, a_ref.shape[2])

    for h in range(2):
        @pl.loop(0, half // chunk)
        def _(j, h=h):
            at = pl.ds(pl.multiple_of(h * half + j * chunk, chunk), chunk)
            to = pl.ds(pl.multiple_of(j * chunk, chunk), chunk)
            r = jnp.dot(heads, wo[:, at], preferred_element_type=f32)
            r = r.reshape(2, 2, 2, 2, rows_dev, chunk)
            even, odd = r[:, :, :, 0], r[:, :, :, 1]
            part[h, :, :, :, :, to] = jnp.where(cc == 0, even, odd)
            part_send[h, :, :, :, :, to] = jnp.where(cc == 0, odd, even).astype(bf16)

        if h == 0:
            pl.semaphore_wait(barrier, len(others))
        send(part_send.at[h], part_recv.at[h], ps.at[h], pr.at[h], core)

    for h in range(2):
        wait(part_send.at[h], part_recv.at[h], ps.at[h], pr.at[h], core)
        if h == 0:
            away = part[0, :, 1 - yy] + part_recv[0, :, 1 - yy].astype(f32)
        else:
            away = part[1, :, :, 1 - xx] + part_recv[1, :, :, 1 - xx].astype(f32)
        t1_send[h] = away.astype(bf16)
        send(t1_send.at[h], t1_recv.at[h], t1s.at[h], t1r.at[h], first_nbr[h])
    keep1[0] = part[0, :, yy] + part_recv[0, :, yy].astype(f32)
    keep1[1] = part[1, :, :, xx] + part_recv[1, :, :, xx].astype(f32)
    for h in range(2):
        wait(t1_send.at[h], t1_recv.at[h], t1s.at[h], t1r.at[h], first_nbr[h])
        at = second_at[h]
        t2_send[h] = (keep1[h, :, 1 - at] + t1_recv[h, :, 1 - at].astype(f32)).astype(bf16)
        send(t2_send.at[h], t2_recv.at[h], t2s.at[h], t2r.at[h], second_nbr[h])
        keep2[h] = keep1[h, :, at] + t1_recv[h, :, at].astype(f32)
    for h in range(2):
        wait(t2_send.at[h], t2_recv.at[h], t2s.at[h], t2r.at[h], second_nbr[h])
        t3_send[h] = (keep2[h, 1 - low] + t2_recv[h, 1 - low].astype(f32)).astype(bf16)
        send(t3_send.at[h], t3_recv.at[h], t3s.at[h], t3r.at[h], znbr)
        state[h] = keep2[h, low] + t2_recv[h, low].astype(f32)
    square = 0.0
    for h in range(2):
        wait(t3_send.at[h], t3_recv.at[h], t3s.at[h], t3r.at[h], znbr)
        total = state[h] + t3_recv[h].astype(f32)
        state[h] = total
        square += jnp.sum(total * total, axis=-1, keepdims=True)
    scale = lax.rsqrt(square / (2 * half) + 1e-06)
    for h in range(2):
        gain = gain_ref[:, h * half:(h + 1) * half].astype(f32)
        rows[q, yy, xx, cc, h, :, 0:half] = (state[h] * scale * gain).astype(bf16)
        rows[q, yy, xx, cc, h, :, half:half + LANES] = dense_ref[h]

    own = rows.at[q, yy, xx, cc]
    for k in range(1, slabs):
        send(own, own, zs.at[k], zr.at[k], slab_at(k) * 8 + inner)

    def first(k):
        s = slab_at(slabs - k)
        block = rows.at[s, yy, xx, cc]
        if k:
            wait(block, block, zs.at[k], zr.at[k], slab_at(k) * 8 + inner)
        send(block, block, fs.at[k, 0], fr.at[k, 0], xnbr)
        send(block, block, fs.at[k, 1], fr.at[k, 1], ynbr)
        send(block, block, cs.at[k, 0], cr.at[k, 0], core)

    def relay(k):
        s = slab_at(slabs - k)
        block = rows.at[s, yy, 1 - xx, cc]
        wait(block, block, fs.at[k, 0], fr.at[k, 0], xnbr)
        send(block.at[0], block.at[0], ds.at[k, 0], dr.at[k, 0], ynbr)
        send(block, block, cs.at[k, 1], cr.at[k, 1], core)
        block = rows.at[s, 1 - yy, xx, cc]
        wait(block, block, fs.at[k, 1], fr.at[k, 1], ynbr)
        send(block.at[1], block.at[1], ds.at[k, 1], dr.at[k, 1], xnbr)
        send(block, block, cs.at[k, 2], cr.at[k, 2], core)

    def corner(k):
        s = slab_at(slabs - k)
        block = rows.at[s, 1 - yy, 1 - xx, cc]
        wait(block.at[0], block.at[0], ds.at[k, 0], dr.at[k, 0], ynbr)
        wait(block.at[1], block.at[1], ds.at[k, 1], dr.at[k, 1], xnbr)
        send(block, block, cs.at[k, 3], cr.at[k, 3], core)

    def expert(k):
        s = slab_at(slabs - k)
        for i, (ay, ax) in enumerate([(yy, xx), (yy, 1 - xx), (1 - yy, xx), (1 - yy, 1 - xx)]):
            block = rows.at[s, ay, ax, 1 - cc]
            wait(block, block, cs.at[k, i], cr.at[k, i], core)
        if k == 0:
            loads[1].wait()
            loads[2].wait()
        count = 8 * rows_dev
        wide = min(256, units)

        @pl.loop(0, 2 * units // wide)
        def _(n):
            at = pl.ds(pl.multiple_of(n * wide, wide), wide)
            total = jnp.dot(rows[s, :, :, :, 0, :, 0:half].reshape(count, half), w[0:half, at],
                            preferred_element_type=f32)
            total += jnp.dot(rows[s, :, :, :, 1, :, 0:half].reshape(count, half),
                             w[half:2 * half, at], preferred_element_type=f32)
            hidden[:, at] = total

        act = (jax.nn.silu(hidden[:, 0:units]) * hidden[:, units:2 * units]).astype(bf16)
        lane = lax.broadcasted_iota(jnp.int32, (count, LANES), 1)
        weight = (rows[s, :, :, :, 0, :, half:half + LANES].astype(f32)
                  + rows[s, :, :, :, 1, :, half:half + LANES].astype(f32)).reshape(count, LANES)
        weight = jnp.sum(jnp.where(lane == me // 2, weight, 0.0), axis=1, keepdims=True)
        if k == 0:
            loads[3].wait()
        for h in range(2):
            @pl.loop(0, half // chunk)
            def _(j, h=h):
                at = pl.ds(pl.multiple_of(h * half + j * chunk, chunk), chunk)
                to = pl.ds(pl.multiple_of(j * chunk, chunk), chunk)
                r = jnp.dot(act, wd[:, at], preferred_element_type=f32) * weight
                r = r.reshape(2, 2, 2, rows_dev, chunk)
                even, odd = r[:, :, 0], r[:, :, 1]
                y[k % y.shape[0], h, :, :, :, to] = jnp.where(cc == 0, even, odd)
                y_send[k, h, :, :, :, to] = jnp.where(cc == 0, odd, even).astype(bf16)
            send(y_send.at[k, h], y_recv.at[k, h], ys.at[k, h], yr.at[k, h], core)

    def sum_core(k):
        i = k % y.shape[0]
        for h in range(2):
            wait(y_send.at[k, h], y_recv.at[k, h], ys.at[k, h], yr.at[k, h], core)
            if h == 0:
                away = y[i, 0, 1 - yy] + y_recv[k, 0, 1 - yy].astype(f32)
            else:
                away = y[i, 1, :, 1 - xx] + y_recv[k, 1, :, 1 - xx].astype(f32)
            v1_send[k, h] = away.astype(bf16)
            send(v1_send.at[k, h], v1_recv.at[k, h], v1s.at[k, h], v1r.at[k, h], first_nbr[h])

    def second(k):
        i = k % y.shape[0]
        for h in range(2):
            wait(v1_send.at[k, h], v1_recv.at[k, h], v1s.at[k, h], v1r.at[k, h], first_nbr[h])
            at = second_at[h]

            def summed(b):
                mid = (yy, b) if h == 0 else (b, xx)
                return (y[i, h, mid[0], mid[1]] + y_recv[k, h, mid[0], mid[1]].astype(f32)
                        + v1_recv[k, h, b].astype(f32))
            v2_send[k, h] = summed(1 - at).astype(bf16)
            send(v2_send.at[k, h], v2_recv.at[k, h], v2s.at[k, h], v2r.at[k, h], second_nbr[h])
            keep3[k, h] = summed(at)

    def home(k):
        for h in range(2):
            wait(v2_send.at[k, h], v2_recv.at[k, h], v2s.at[k, h], v2r.at[k, h], second_nbr[h])
            total = keep3[k, h] + v2_recv[k, h].astype(f32)
            if k:
                v3_send[k, h] = total.astype(bf16)
            else:
                state[h] = state[h] + total
        if k:
            send(v3_send.at[k], v3_recv.at[k], v3s.at[k], v3r.at[k], slab_at(slabs - k) * 8 + inner)

    steps = {"first": first, "relay": relay, "corner": corner, "expert": expert, "sum": sum_core,
             "second": second, "home": home}
    order = sorted((k * STRIDE + OFFSETS[name], -OFFSETS[name], k, name)
                   for k in range(slabs) for name in steps)
    for _, _, k, name in order:
        steps[name](k)
    for k in range(1, slabs):
        wait(v3_send.at[k], v3_recv.at[k], v3s.at[k], v3r.at[k], slab_at(k) * 8 + inner)
    for h in range(2):
        total = state[h]
        for k in range(1, slabs):
            total = total + v3_recv[k, h].astype(f32)
        out_ref[:, h * half:(h + 1) * half] = total.astype(bf16)
    for made in sent:
        made.wait_send()


def body(attn_heads, out_proj, norm_gain, routes, gate_weights, expert_home, w_gate, w_up, w_down):
    width = out_proj.shape[2]
    rows_dev = routes.shape[0]
    units = w_down.shape[1]
    slabs = lax.axis_size("expert") // 8
    half = width // 2
    bf16, f32 = jnp.bfloat16, jnp.float32
    named = routes[:, :, None] == jnp.arange(expert_home.shape[0], dtype=jnp.int32)
    homes = jnp.sum(jnp.where(named, expert_home, 0), axis=2)
    at = homes[:, :, None] == jnp.arange(LANES, dtype=jnp.int32)
    dense = jnp.sum(jnp.where(at, gate_weights[:, :, None], 0.0), axis=1)
    coarse = lax.reduce_precision(dense, 8, 7)
    dense = jnp.stack([coarse, dense - coarse]).astype(bf16)
    heads = attn_heads[0].reshape(16, rows_dev, attn_heads.shape[2])
    vmem, dma = pltpu.VMEM, pltpu.SemaphoreType.DMA
    blk = (rows_dev, half)
    ring = min(slabs, 4)
    scratch = [
        vmem(out_proj.shape[1:], bf16), vmem((width, 2 * units), bf16), vmem((units, width), bf16),
        vmem((2, 2, 2, 2) + blk, f32), vmem((2, 2, 2, 2) + blk, bf16), vmem((2, 2, 2, 2) + blk, bf16),
        vmem((2, 2, 2) + blk, bf16), vmem((2, 2, 2) + blk, bf16), vmem((2, 2, 2) + blk, f32),
        vmem((2, 2) + blk, bf16), vmem((2, 2) + blk, bf16), vmem((2, 2) + blk, f32),
        vmem((2,) + blk, bf16), vmem((2,) + blk, bf16), vmem((2,) + blk, f32),
        vmem((slabs, 2, 2, 2, 2, rows_dev, half + LANES), bf16),
        vmem((8 * rows_dev, 2 * units), f32),
        vmem((ring, 2, 2, 2) + blk, f32),
        vmem((slabs, 2, 2, 2) + blk, bf16), vmem((slabs, 2, 2, 2) + blk, bf16),
        vmem((slabs, 2, 2) + blk, bf16), vmem((slabs, 2, 2) + blk, bf16),
        vmem((slabs, 2) + blk, bf16), vmem((slabs, 2) + blk, bf16),
        vmem((slabs, 2) + blk, f32),
        vmem((slabs, 2) + blk, bf16), vmem((slabs, 2) + blk, bf16),
        dma((4,)),
    ]
    for shape in [(2,)] * 4 + [(slabs,)] + [(slabs, 2)] * 2 + [(slabs, 4)] + [(slabs, 2)] * 3 + [(slabs,)]:
        scratch += [dma(shape), dma(shape)]
    inside = pl.BlockSpec(memory_space=pltpu.VMEM)
    outside = pl.BlockSpec(memory_space=pl.ANY)
    return pl.pallas_call(
        functools.partial(kernel, slabs),
        out_shape=jax.ShapeDtypeStruct((rows_dev, width), bf16),
        in_specs=[inside, outside, inside, inside, outside, outside, outside],
        out_specs=inside,
        scratch_shapes=scratch,
        compiler_params=pltpu.CompilerParams(
            collective_id=0, has_side_effects=True, vmem_limit_bytes=60 * 2**20
        ),
    )(heads, out_proj[0], norm_gain[None, :], dense, w_gate[0], w_up[0], w_down[0])


def solution(mesh):
    placed = (
        P(("groups", "expert"), None, None),
        P("expert", None, None),
        P(),
        P(("groups", "expert"), None),
        P(("groups", "expert"), None),
        P(),
        P("expert", None, None),
        P("expert", None, None),
        P("expert", None, None),
    )
    return jax.shard_map(
        body, mesh=mesh, in_specs=placed, out_specs=P(("groups", "expert"), None), check_vma=False
    )
```

time: 300 us -> 90.4 us (0.30)
  waiting for transfers between devices: 222 us -> 0 us
  Pallas kernels: 0 us -> 83.9 us
  blocking collectives: 39 us -> 0 us
  matrix products: 20 us -> 0 us
  between operations: 13.2 us -> 0.03 us
  local copies, waits for them, and re-layouts: 0.17 us -> 4.4 us
    reduce_scatter x2 -> x0, waiting for transfers between devices: 201 us -> none  [the longest x1 139 us: body(): lax.psum_scatter(part.astype(jnp.bfloat16), 'expert', scatter_dimension=0...]
    pallas_call x0 -> x1, Pallas kernels: none -> 83.9 us  [body(): pl.pallas_call(functools.partial(kernel, slabs), out_shape=jax.ShapeDtype...]
    all_gather x1 -> x0, blocking collectives: 39 us -> none  [body(): dense = lax.all_gather(dense, 'expert', axis=0, tiled=True)]
    all_gather x1 -> x0, waiting for transfers between devices: 21.3 us -> none  [body(): rows = lax.all_gather(normed, 'expert', axis=0, tiled=True)]
    dot_general x3 -> x0, matrix products: 20 us -> none  [the longest x1 9.73 us: body(): jnp.dot(act, w_down[0], preferred_element_type=jnp.float32) * gate_here]
    convert_element_type x3 -> x0, other arithmetic: 3.27 us -> none  [the longest x1 1.66 us: body(): (state * scale * norm_gain.astype(jnp.float32)).astype(jnp.bfloat16)]
  transfers between devices with their start and end apart: 3 -> 0, of which waited for: 3 -> 0; matrix products, arithmetic and copies ran while one was open for 0% -> 0% of each run, Pallas kernels for 0% -> 0%
where the time goes in v2:
time: 90.4 us; the launch traced here: 90.1 us
  Pallas kernels  83.9 us (93%)
  local copies, waits for them, and re-layouts  4.4 us (5%)
  other arithmetic  1.78 us (2%)
    pallas_call x1, Pallas kernels, body(): pl.pallas_call(functools.partial(kernel, slabs), out_shape=jax.ShapeDtype...  83.9 us
    unnamed x3, local copies, waits for them, and re-layouts  3.09 us

profile of v2, /device:TPU:0, one launch (start us, length us, event | category | flops | bytes accessed | tf_op | source)
XLA Modules:
  0.0 90.1 jit_solution(11031264220710921787)
XLA Ops:
  0.0 0.8 copy.12
  0.8 1.1 %select_reduce_fusion.1 = s32[16,8]{1,0:T(8,128)S(1)} fusion(s32[16]{0:T(128)} %param.14, s32[16,8]{1,0:T(8,128)S(1)} %copy.12), kind=kLoop, calls=%fused_computation.2 | loop fusion | flops 6016 | bytes 1088 | tf_op jit(solution)/shard_map/reduce_sum | solution.py:251
  1.8 0.8 copy.13
  2.6 0.1 select_reduce_fusion
  2.7 0.6 pad_maximum_fusion.dense_ref
  3.3 1.3 %broadcast_in_dim.28.gain_ref = bf16[1,4096]{1,0:T(2,128)(2,1)} reshape(bf16[4096]{0:T(1024)(128)(2,1)} %param.11) | data formatting | bytes 16384 | tf_op jit(solution)/shard_map/broadcast_in_dim | solution.py:289
  4.6 83.9 %shard_map.91 = bf16[16,4096]{1,0:T(8,128)(2,1)} custom-call(bf16[16,16,256]{2,1,0:T(8,128)(2,1)} %bitcast.12, bf16[256,4096]{1,0:T(8,128)(2,1)} %bitcast.11, bf16[1,4096]{1,0:T(2,128)(2,1)} %broadcast_in_dim.28.gain_ref, bf16[2,16,128]{2,1,0:T(8,128)(2,1)} %pad_maximum_fusion.dense_ref, bf16[4096,384]{1,0:T(8,128)(2,1)} %bitcast.8, ...), custom_call_target="tpu_custom_call" | custom-call | tf_op jit(solution)/shard_map/pallas_call | solution.py:280
  88.6 1.6 %copy.15 = bf16[16,4096]{1,0:T(8,128)(2,1)} copy(bf16[16,4096]{1,0:T(8,128)(2,1)} %shard_map.91) | data formatting | bytes 262144
  (1 shorter events, 0.0 us)

commit v3 on v2

--- a/solution.py
+++ b/solution.py
@@ -7,14 +7,22 @@
 from jax.sharding import PartitionSpec as P
 
 LANES = 128
-STRIDE = 2
-OFFSETS = {"first": 0, "relay": 1, "corner": 2, "expert": 3, "sum": 4, "second": 5, "home": 6}
-
-
-def kernel(slabs, a_ref, wo_hbm, gain_ref, dense_ref, wg_hbm, wu_hbm, wd_hbm, out_ref, wo, w, wd,
-           part, part_send, part_recv, t1_send, t1_recv, keep1, t2_send, t2_recv, keep2, t3_send,
-           t3_recv, state, rows, hidden, y, y_send, y_recv, v1_send, v1_recv, v2_send, v2_recv,
-           keep3, v3_send, v3_recv, load_sem, ps, pr, t1s, t1r, t2s, t2r, t3s, t3r, zs, zr, fs, fr,
+PLAN = {"first": (1, 0), "relay": (1, 1), "corner": (1, 2), "expert": (1, 3), "sum": (1, 4),
+        "second": (1, 5), "home": (1, 6)}
+PEERS = (7, 6, 5, 3, 4, 2, 1)
+
+
+def flip(value, mask):
+    for bit in range(mask.bit_length()):
+        if mask >> bit & 1:
+            value = value + (1 << bit) - (2 << bit) * ((value // (1 << bit)) % 2)
+    return value
+
+
+def kernel(slabs, home_ref, a_hbm, wo_hbm, gain_hbm, routes_hbm, gates_hbm, wg_hbm, wu_hbm, wd_hbm,
+           out_ref, a_ref, gain_ref, routes_ref, gates_ref, wo, w, wd, part, part_send, part_recv,
+           group_send, group_recv, state, rows, hidden, y, y_send, y_recv, v1_send, v1_recv,
+           v2_send, v2_recv, keep3, v3_send, v3_recv, load_sem, ps, pr, gs, gr, zs, zr, fs, fr,
            ds, dr, cs, cr, ys, yr, v1s, v1r, v2s, v2r, v3s, v3r):
     f32, bf16 = jnp.float32, jnp.bfloat16
     me = lax.axis_index("expert")
@@ -27,7 +35,6 @@
     core = me + 1 - 2 * cc
     xnbr = me + 2 - 4 * xx
     ynbr = me + 4 - 8 * yy
-    znbr = me + 8 - 16 * low
     half = wo.shape[1] // 2
     units = wd.shape[0]
     rows_dev = out_ref.shape[0]
@@ -37,15 +44,20 @@
     loads = [pltpu.make_async_copy(wo_hbm, wo, load_sem.at[0]),
              pltpu.make_async_copy(wg_hbm, w.at[:, 0:units], load_sem.at[1]),
              pltpu.make_async_copy(wu_hbm, w.at[:, units:2 * units], load_sem.at[2]),
-             pltpu.make_async_copy(wd_hbm, wd, load_sem.at[3])]
-    for load in loads:
-        load.start()
+             pltpu.make_async_copy(wd_hbm, wd, load_sem.at[3]),
+             pltpu.make_async_copy(a_hbm, a_ref, load_sem.at[4]),
+             pltpu.make_async_copy(gain_hbm, gain_ref, load_sem.at[5]),
+             pltpu.make_async_copy(routes_hbm, routes_ref, load_sem.at[6]),
+             pltpu.make_async_copy(gates_hbm, gates_ref, load_sem.at[7])]
+    for i in (4, 0, 6, 7, 5, 1, 2, 3):
+        loads[i].start()
 
     def slab_at(k):
-        return lax.rem(q + k, slabs)
+        return flip(q, k)
 
     barrier = pltpu.get_barrier_semaphore()
-    others = [core, xnbr, ynbr] + [slab_at(k) * 8 + inner for k in range(1, slabs)]
+    others = ([core] + [flip(me, 2 * i) for i in PEERS]
+              + [slab_at(k) * 8 + inner for k in range(2, slabs)])
     for other in others:
         pl.semaphore_signal(barrier, inc=1, device_id={"expert": other},
                             device_id_type=pl.DeviceIdType.MESH)
@@ -65,6 +77,20 @@
     def wait(*args):
         copy(*args).wait_recv()
 
+    loads[6].wait()
+    loads[7].wait()
+    homes = jnp.zeros(routes_ref.shape, jnp.int32)
+    for e in range(home_ref.shape[0]):
+        homes = jnp.where(routes_ref[...] == e, home_ref[e], homes)
+    at_pair = lax.broadcasted_iota(jnp.int32, (LANES, rows_dev), 0)
+    dense = jnp.zeros((LANES, rows_dev), f32)
+    for i in range(routes_ref.shape[0]):
+        dense += jnp.where(homes[i:i + 1] == at_pair, gates_ref[i:i + 1, :], 0.0)
+    dense = dense.T
+    coarse = dense.astype(bf16)
+    rows[q, yy, xx, cc, 0, :, half:half + LANES] = coarse
+    rows[q, yy, xx, cc, 1, :, half:half + LANES] = (dense - coarse.astype(f32)).astype(bf16)
+    loads[4].wait()
     loads[0].wait()
     chunk = min(512, half)
     heads = a_ref[...].reshape(16 * rows_dev, a_ref.shape[2])
@@ -86,43 +112,33 @@
 
     for h in range(2):
         wait(part_send.at[h], part_recv.at[h], ps.at[h], pr.at[h], core)
-        if h == 0:
-            away = part[0, :, 1 - yy] + part_recv[0, :, 1 - yy].astype(f32)
-        else:
-            away = part[1, :, :, 1 - xx] + part_recv[1, :, :, 1 - xx].astype(f32)
-        t1_send[h] = away.astype(bf16)
-        send(t1_send.at[h], t1_recv.at[h], t1s.at[h], t1r.at[h], first_nbr[h])
-    keep1[0] = part[0, :, yy] + part_recv[0, :, yy].astype(f32)
-    keep1[1] = part[1, :, :, xx] + part_recv[1, :, :, xx].astype(f32)
-    for h in range(2):
-        wait(t1_send.at[h], t1_recv.at[h], t1s.at[h], t1r.at[h], first_nbr[h])
-        at = second_at[h]
-        t2_send[h] = (keep1[h, :, 1 - at] + t1_recv[h, :, 1 - at].astype(f32)).astype(bf16)
-        send(t2_send.at[h], t2_recv.at[h], t2s.at[h], t2r.at[h], second_nbr[h])
-        keep2[h] = keep1[h, :, at] + t1_recv[h, :, at].astype(f32)
-    for h in range(2):
-        wait(t2_send.at[h], t2_recv.at[h], t2s.at[h], t2r.at[h], second_nbr[h])
-        t3_send[h] = (keep2[h, 1 - low] + t2_recv[h, 1 - low].astype(f32)).astype(bf16)
-        send(t3_send.at[h], t3_recv.at[h], t3s.at[h], t3r.at[h], znbr)
-        state[h] = keep2[h, low] + t2_recv[h, low].astype(f32)
+        for i, mask in enumerate(PEERS):
+            at = (h, flip(low, mask >> 2), flip(yy, mask >> 1 & 1), flip(xx, mask & 1))
+            group_send[h, i] = (part[at] + part_recv[at].astype(f32)).astype(bf16)
+            send(group_send.at[h, i], group_recv.at[h, i], gs.at[h, i], gr.at[h, i], flip(me, 2 * mask))
+        state[h] = part[h, low, yy, xx] + part_recv[h, low, yy, xx].astype(f32)
     square = 0.0
     for h in range(2):
-        wait(t3_send.at[h], t3_recv.at[h], t3s.at[h], t3r.at[h], znbr)
-        total = state[h] + t3_recv[h].astype(f32)
+        total = state[h]
+        for i, mask in reversed(tuple(enumerate(PEERS))):
+            wait(group_send.at[h, i], group_recv.at[h, i], gs.at[h, i], gr.at[h, i], flip(me, 2 * mask))
+            total += group_recv[h, i].astype(f32)
         state[h] = total
         square += jnp.sum(total * total, axis=-1, keepdims=True)
     scale = lax.rsqrt(square / (2 * half) + 1e-06)
-    for h in range(2):
-        gain = gain_ref[:, h * half:(h + 1) * half].astype(f32)
-        rows[q, yy, xx, cc, h, :, 0:half] = (state[h] * scale * gain).astype(bf16)
-        rows[q, yy, xx, cc, h, :, half:half + LANES] = dense_ref[h]
+    loads[5].wait()
+    gain = gain_ref[...].astype(f32)
+    for i in range(2 * half // LANES):
+        h, to = i * LANES // half, i * LANES % half
+        rows[q, yy, xx, cc, h, :, to:to + LANES] = (
+            state[h, :, to:to + LANES] * scale * gain[i:i + 1]).astype(bf16)
 
     own = rows.at[q, yy, xx, cc]
     for k in range(1, slabs):
         send(own, own, zs.at[k], zr.at[k], slab_at(k) * 8 + inner)
 
     def first(k):
-        s = slab_at(slabs - k)
+        s = slab_at(k)
         block = rows.at[s, yy, xx, cc]
         if k:
             wait(block, block, zs.at[k], zr.at[k], slab_at(k) * 8 + inner)
@@ -131,7 +147,7 @@
         send(block, block, cs.at[k, 0], cr.at[k, 0], core)
 
     def relay(k):
-        s = slab_at(slabs - k)
+        s = slab_at(k)
         block = rows.at[s, yy, 1 - xx, cc]
         wait(block, block, fs.at[k, 0], fr.at[k, 0], xnbr)
         send(block.at[0], block.at[0], ds.at[k, 0], dr.at[k, 0], ynbr)
@@ -142,14 +158,14 @@
         send(block, block, cs.at[k, 2], cr.at[k, 2], core)
 
     def corner(k):
-        s = slab_at(slabs - k)
+        s = slab_at(k)
         block = rows.at[s, 1 - yy, 1 - xx, cc]
         wait(block.at[0], block.at[0], ds.at[k, 0], dr.at[k, 0], ynbr)
         wait(block.at[1], block.at[1], ds.at[k, 1], dr.at[k, 1], xnbr)
         send(block, block, cs.at[k, 3], cr.at[k, 3], core)
 
     def expert(k):
-        s = slab_at(slabs - k)
+        s = slab_at(k)
         for i, (ay, ax) in enumerate([(yy, xx), (yy, 1 - xx), (1 - yy, xx), (1 - yy, 1 - xx)]):
             block = rows.at[s, ay, ax, 1 - cc]
             wait(block, block, cs.at[k, i], cr.at[k, i], core)
@@ -221,11 +237,11 @@
             else:
                 state[h] = state[h] + total
         if k:
-            send(v3_send.at[k], v3_recv.at[k], v3s.at[k], v3r.at[k], slab_at(slabs - k) * 8 + inner)
+            send(v3_send.at[k], v3_recv.at[k], v3s.at[k], v3r.at[k], slab_at(k) * 8 + inner)
 
     steps = {"first": first, "relay": relay, "corner": corner, "expert": expert, "sum": sum_core,
              "second": second, "home": home}
-    order = sorted((k * STRIDE + OFFSETS[name], -OFFSETS[name], k, name)
+    order = sorted((k * PLAN[name][0] + PLAN[name][1], -PLAN[name][1], k, name)
                    for k in range(slabs) for name in steps)
     for _, _, k, name in order:
         steps[name](k)
@@ -247,22 +263,16 @@
     slabs = lax.axis_size("expert") // 8
     half = width // 2
     bf16, f32 = jnp.bfloat16, jnp.float32
-    named = routes[:, :, None] == jnp.arange(expert_home.shape[0], dtype=jnp.int32)
-    homes = jnp.sum(jnp.where(named, expert_home, 0), axis=2)
-    at = homes[:, :, None] == jnp.arange(LANES, dtype=jnp.int32)
-    dense = jnp.sum(jnp.where(at, gate_weights[:, :, None], 0.0), axis=1)
-    coarse = lax.reduce_precision(dense, 8, 7)
-    dense = jnp.stack([coarse, dense - coarse]).astype(bf16)
     heads = attn_heads[0].reshape(16, rows_dev, attn_heads.shape[2])
     vmem, dma = pltpu.VMEM, pltpu.SemaphoreType.DMA
     blk = (rows_dev, half)
     ring = min(slabs, 4)
     scratch = [
+        vmem(heads.shape, bf16), vmem((width // LANES, LANES), bf16), vmem(routes.shape[::-1], jnp.int32),
+        vmem(routes.shape[::-1], f32),
         vmem(out_proj.shape[1:], bf16), vmem((width, 2 * units), bf16), vmem((units, width), bf16),
         vmem((2, 2, 2, 2) + blk, f32), vmem((2, 2, 2, 2) + blk, bf16), vmem((2, 2, 2, 2) + blk, bf16),
-        vmem((2, 2, 2) + blk, bf16), vmem((2, 2, 2) + blk, bf16), vmem((2, 2, 2) + blk, f32),
-        vmem((2, 2) + blk, bf16), vmem((2, 2) + blk, bf16), vmem((2, 2) + blk, f32),
-        vmem((2,) + blk, bf16), vmem((2,) + blk, bf16), vmem((2,) + blk, f32),
+        vmem((2, 7) + blk, bf16), vmem((2, 7) + blk, bf16), vmem((2,) + blk, f32),
         vmem((slabs, 2, 2, 2, 2, rows_dev, half + LANES), bf16),
         vmem((8 * rows_dev, 2 * units), f32),
         vmem((ring, 2, 2, 2) + blk, f32),
@@ -271,22 +281,23 @@
         vmem((slabs, 2) + blk, bf16), vmem((slabs, 2) + blk, bf16),
         vmem((slabs, 2) + blk, f32),
         vmem((slabs, 2) + blk, bf16), vmem((slabs, 2) + blk, bf16),
-        dma((4,)),
+        dma((8,)),
     ]
-    for shape in [(2,)] * 4 + [(slabs,)] + [(slabs, 2)] * 2 + [(slabs, 4)] + [(slabs, 2)] * 3 + [(slabs,)]:
+    for shape in [(2,), (2, 7), (slabs,)] + [(slabs, 2)] * 2 + [(slabs, 4)] + [(slabs, 2)] * 3 + [(slabs,)]:
         scratch += [dma(shape), dma(shape)]
     inside = pl.BlockSpec(memory_space=pltpu.VMEM)
     outside = pl.BlockSpec(memory_space=pl.ANY)
     return pl.pallas_call(
         functools.partial(kernel, slabs),
         out_shape=jax.ShapeDtypeStruct((rows_dev, width), bf16),
-        in_specs=[inside, outside, inside, inside, outside, outside, outside],
+        in_specs=[pl.BlockSpec(memory_space=pltpu.SMEM)] + [outside] * 8,
         out_specs=inside,
         scratch_shapes=scratch,
         compiler_params=pltpu.CompilerParams(
             collective_id=0, has_side_effects=True, vmem_limit_bytes=60 * 2**20
         ),
-    )(heads, out_proj[0], norm_gain[None, :], dense, w_gate[0], w_up[0], w_down[0])
+    )(expert_home, heads, out_proj[0], norm_gain.reshape(width // LANES, LANES), routes.T,
+      gate_weights.T, w_gate[0], w_up[0], w_down[0])
 
 
 def solution(mesh):

time: 90.4 us -> 79 us (0.87)
  Pallas kernels: 83.9 us -> 77.3 us
  local copies, waits for them, and re-layouts: 4.4 us -> 1.57 us
  other arithmetic: 1.78 us -> 0 us
    pallas_call x1, Pallas kernels: 83.9 us -> 77.3 us  [body(): pl.pallas_call(functools.partial(kernel, slabs), out_shape=jax.ShapeDtype...]
    unnamed x3 -> x1, local copies, waits for them, and re-layouts: 3.09 us -> 1.57 us
    broadcast_in_dim x1 -> x0, local copies, waits for them, and re-layouts: 1.31 us -> none  [body(): norm_gain[None, :]]
    reduce_sum x2 -> x0, other arithmetic: 1.17 us -> none  [the longest x1 1.07 us: body(): homes = jnp.sum(jnp.where(named, expert_home, 0), axis=2)]
where the time goes in v3:
time: 79 us; the launch traced here: 78.8 us
  Pallas kernels  77.3 us (98%)
  local copies, waits for them, and re-layouts  1.57 us (2%)
    pallas_call x1, Pallas kernels, body(): pl.pallas_call(functools.partial(kernel, slabs), out_shape=jax.ShapeDtype...  77.3 us

profile of v3, /device:TPU:0, one launch (start us, length us, event | category | flops | bytes accessed | tf_op | source)
XLA Modules:
  0.0 78.8 jit_solution(8337993868919918590)
XLA Ops:
  0.0 77.3 %shard_map.91 = bf16[16,4096]{1,0:T(8,128)(2,1)} custom-call(s32[16]{0:T(128)} %home_ref.1, bf16[16,16,256]{2,1,0:T(8,128)(2,1)} %bitcast.12, bf16[256,4096]{1,0:T(8,128)(2,1)} %bitcast.11, bf16[32,128]{1,0:T(8,128)(2,1)} %bitcast.13, s32[8,16]{1,0:T(8,128)} %bitcast.14, f32[8,16]{1,0:T(8,128)} %bitcast.15, bf16[4096,384]{1,0:T(8,128)(2,1)} %bitcast.8, ...), custom_call_target="tpu_custom_call" | custom-call | tf_op jit(solution)/shard_map/pallas_call | solution.py:290
  77.3 1.6 %copy.11 = bf16[16,4096]{1,0:T(8,128)(2,1)} copy(bf16[16,4096]{1,0:T(8,128)(2,1)} %shard_map.91) | data formatting | bytes 262144

commit v4 on v3

--- a/solution.py
+++ b/solution.py
@@ -7,8 +7,9 @@
 from jax.sharding import PartitionSpec as P
 
 LANES = 128
-PLAN = {"first": (1, 0), "relay": (1, 1), "corner": (1, 2), "expert": (1, 3), "sum": (1, 4),
-        "second": (1, 5), "home": (1, 6)}
+PLAN = {'first': (1, -0.5), 'relay': (1, 1), 'corner': (1, 2), 'expert': (1, 3), 'sum': (1, 4), 'second': (1, 5), 'home': (1, 6)}
+GATHER_DIRECT = ()
+SUM_DIRECT = ()
 PEERS = (7, 6, 5, 3, 4, 2, 1)
 
 
@@ -133,35 +134,42 @@
         rows[q, yy, xx, cc, h, :, to:to + LANES] = (
             state[h, :, to:to + LANES] * scale * gain[i:i + 1]).astype(bf16)
 
-    own = rows.at[q, yy, xx, cc]
-    for k in range(1, slabs):
-        send(own, own, zs.at[k], zr.at[k], slab_at(k) * 8 + inner)
-
     def first(k):
         s = slab_at(k)
         block = rows.at[s, yy, xx, cc]
         if k:
             wait(block, block, zs.at[k], zr.at[k], slab_at(k) * 8 + inner)
+        bit = 1
+        while bit < (k & -k if k else slabs):
+            send(block, block, zs.at[k + bit], zr.at[k + bit], slab_at(bit) * 8 + inner)
+            bit *= 2
         send(block, block, fs.at[k, 0], fr.at[k, 0], xnbr)
         send(block, block, fs.at[k, 1], fr.at[k, 1], ynbr)
+        if k in GATHER_DIRECT:
+            send(block, block, ds.at[k, 0], dr.at[k, 0], flip(me, 6))
         send(block, block, cs.at[k, 0], cr.at[k, 0], core)
 
     def relay(k):
         s = slab_at(k)
         block = rows.at[s, yy, 1 - xx, cc]
         wait(block, block, fs.at[k, 0], fr.at[k, 0], xnbr)
-        send(block.at[0], block.at[0], ds.at[k, 0], dr.at[k, 0], ynbr)
+        if k not in GATHER_DIRECT:
+            send(block.at[0], block.at[0], ds.at[k, 0], dr.at[k, 0], ynbr)
         send(block, block, cs.at[k, 1], cr.at[k, 1], core)
         block = rows.at[s, 1 - yy, xx, cc]
         wait(block, block, fs.at[k, 1], fr.at[k, 1], ynbr)
-        send(block.at[1], block.at[1], ds.at[k, 1], dr.at[k, 1], xnbr)
+        if k not in GATHER_DIRECT:
+            send(block.at[1], block.at[1], ds.at[k, 1], dr.at[k, 1], xnbr)
         send(block, block, cs.at[k, 2], cr.at[k, 2], core)
 
     def corner(k):
         s = slab_at(k)
         block = rows.at[s, 1 - yy, 1 - xx, cc]
-        wait(block.at[0], block.at[0], ds.at[k, 0], dr.at[k, 0], ynbr)
-        wait(block.at[1], block.at[1], ds.at[k, 1], dr.at[k, 1], xnbr)
+        if k in GATHER_DIRECT:
+            wait(block, block, ds.at[k, 0], dr.at[k, 0], flip(me, 6))
+        else:
+            wait(block.at[0], block.at[0], ds.at[k, 0], dr.at[k, 0], ynbr)
+            wait(block.at[1], block.at[1], ds.at[k, 1], dr.at[k, 1], xnbr)
         send(block, block, cs.at[k, 3], cr.at[k, 3], core)
 
     def expert(k):
@@ -203,8 +211,32 @@
                 y_send[k, h, :, :, :, to] = jnp.where(cc == 0, odd, even).astype(bf16)
             send(y_send.at[k, h], y_recv.at[k, h], ys.at[k, h], yr.at[k, h], core)
 
+    def straight(k):
+        return ((v1_send.at[k, 0], v1_recv.at[k, 0], v1s.at[k, 0], v1r.at[k, 0], xnbr),
+                (v1_send.at[k, 1], v1_recv.at[k, 1], v1s.at[k, 1], v1r.at[k, 1], ynbr),
+                (v2_send.at[k], v2_recv.at[k], v2s.at[k, 0], v2r.at[k, 0], flip(me, 6)))
+
     def sum_core(k):
         i = k % y.shape[0]
+        if k in SUM_DIRECT:
+            for h in range(2):
+                wait(y_send.at[k, h], y_recv.at[k, h], ys.at[k, h], yr.at[k, h], core)
+
+            def summed(h, ay, ax):
+                return (y[i, h, ay, ax] + y_recv[k, h, ay, ax].astype(f32)).astype(bf16)
+            hops = straight(k)
+            for h in range(2):
+                v2_send[k, h] = summed(h, 1 - yy, 1 - xx)
+            send(*hops[2])
+            for h in range(2):
+                v1_send[k, 0, h] = summed(h, yy, 1 - xx)
+            send(*hops[0])
+            for h in range(2):
+                v1_send[k, 1, h] = summed(h, 1 - yy, xx)
+            send(*hops[1])
+            for h in range(2):
+                keep3[k, h] = y[i, h, yy, xx] + y_recv[k, h, yy, xx].astype(f32)
+            return
         for h in range(2):
             wait(y_send.at[k, h], y_recv.at[k, h], ys.at[k, h], yr.at[k, h], core)
             if h == 0:
@@ -216,6 +248,8 @@
 
     def second(k):
         i = k % y.shape[0]
+        if k in SUM_DIRECT:
+            return
         for h in range(2):
             wait(v1_send.at[k, h], v1_recv.at[k, h], v1s.at[k, h], v1r.at[k, h], first_nbr[h])
             at = second_at[h]
@@ -229,9 +263,16 @@
             keep3[k, h] = summed(at)
 
     def home(k):
+        if k in SUM_DIRECT:
+            for hop in straight(k):
+                wait(*hop)
         for h in range(2):
-            wait(v2_send.at[k, h], v2_recv.at[k, h], v2s.at[k, h], v2r.at[k, h], second_nbr[h])
-            total = keep3[k, h] + v2_recv[k, h].astype(f32)
+            if k in SUM_DIRECT:
+                total = (keep3[k, h] + v2_recv[k, h].astype(f32) + v1_recv[k, 0, h].astype(f32)
+                         + v1_recv[k, 1, h].astype(f32))
+            else:
+                wait(v2_send.at[k, h], v2_recv.at[k, h], v2s.at[k, h], v2r.at[k, h], second_nbr[h])
+                total = keep3[k, h] + v2_recv[k, h].astype(f32)
             if k:
                 v3_send[k, h] = total.astype(bf16)
             else:

time: 79 us -> 77.9 us (0.986)
  Pallas kernels: 77.3 us -> 76.2 us
    pallas_call x1, Pallas kernels: 77.3 us -> 76.2 us  [body(): pl.pallas_call(functools.partial(kernel, slabs), out_shape=jax.ShapeDtype...]
where the time goes in v4:
time: 77.9 us; the launch traced here: 77.7 us
  Pallas kernels  76.2 us (98%)
  local copies, waits for them, and re-layouts  1.57 us (2%)
    pallas_call x1, Pallas kernels, body(): pl.pallas_call(functools.partial(kernel, slabs), out_shape=jax.ShapeDtype...  76.2 us
    unnamed x1, local copies, waits for them, and re-layouts  1.57 us

profile of v4, /device:TPU:0, one launch (start us, length us, event | category | flops | bytes accessed | tf_op | source)
XLA Modules:
  0.0 77.7 jit_solution(10025867646026973393)
XLA Ops:
  0.0 76.2 %shard_map.91 = bf16[16,4096]{1,0:T(8,128)(2,1)} custom-call(s32[16]{0:T(128)} %home_ref.1, bf16[16,16,256]{2,1,0:T(8,128)(2,1)} %bitcast.12, bf16[256,4096]{1,0:T(8,128)(2,1)} %bitcast.11, bf16[32,128]{1,0:T(8,128)(2,1)} %bitcast.13, s32[8,16]{1,0:T(8,128)} %bitcast.14, f32[8,16]{1,0:T(8,128)} %bitcast.15, bf16[4096,384]{1,0:T(8,128)(2,1)} %bitcast.8, ...), custom_call_target="tpu_custom_call" | custom-call | tf_op jit(solution)/shard_map/pallas_call | solution.py:331
  76.2 1.6 %copy.11 = bf16[16,4096]{1,0:T(8,128)(2,1)} copy(bf16[16,4096]{1,0:T(8,128)(2,1)} %shard_map.91) | data formatting | bytes 262144
